TPU v7x, 256 devices: a whole 4x4x8 slice. The times are simulated.
256 devices in a mesh: illum: 8 (over z), box: 32 (over x, y, core).
Axes of the slice: x: 4, y: 4, z: 8, core: 2. Of those that a mesh axis runs over, the one named last changes fastest.
Arguments:
- patterns: bfloat16 [2, 512, 128, 1024], P(None, 'box', None, 'illum'), parts along dimension 3, may hold values from -6 to 6
- owner_block: int32 [4], replicated, may hold values from 0 to 63
- low_index: int32 [512, 48], P('box'), may hold values from 0 to 315
- low_mask: int32 [512, 48], P('box'), may hold values 0 or 1
- low_table: bfloat16 [2, 316, 128], replicated, may hold values from -2 to 2
- interp: bfloat16 [128, 512], replicated, may hold values from -0.5 to 0.5
- shift_angle: float32 [8, 512], replicated, may hold values from -3.140625 to 3.140625
- par_source: int32 [64, 16], replicated, may hold values from 0 to 63, as said below
- par_index: int32 [64, 16], replicated, may hold values from 0 to 315
- par_mask: int32 [64, 16], replicated, may hold values 0 or 1
- par_table: bfloat16 [2, 316, 512], replicated, may hold values from -1.5 to 1.5
Outputs:
- incoming: float32 [2, 512, 128, 1024], P(None, 'box', None, 'illum'), parts along dimension 3
There are 8 independent parts, one for each index of `illum`. A program takes and returns all parts, laid end to end along the dimension named above; an argument that names none is the same for every part. Nothing has to cross between parts.
Inputs may be any that keep to these rules, and one draw needn't show every extreme that they name: `par_source`: each parent's 16 slots name distinct parents other than itself.
All inputs are finite; a program needn't handle non-finite values. No bound on the sum of `low_mask` on one device may be relied on, other than what follows from the above.
Results may differ from a plain program's by a relative error of at most 0.0047.
Values may be sent and summed in bfloat16 or wider, within the bound.
No kernel may reach another device: no remote copies, remote signals or barrier semaphores. Data moves between devices by JAX's collectives and lax.ppermute only.
A program may use at most 64 MiB of HBM per device.

v0:
```python
import jax
import jax.numpy as jnp
from jax import lax
from jax.sharding import PartitionSpec as P


def broadcast(x, axis, root):
    mine = lax.axis_index(axis) == root
    return lax.psum(jnp.where(mine, x, jnp.zeros_like(x)), axis)


def complex_apply(operator, sources):

    def single(left, right):
        return jnp.einsum("bjk,jkr->bkr", left, right, preferred_element_type=jnp.float32)

    real_part = single(operator[0], sources[0]) - single(operator[1], sources[1])
    imaginary = single(operator[0], sources[1]) + single(operator[1], sources[0])
    return jnp.stack([real_part, imaginary])


def shards(
    patterns,
    owner_block,
    low_index,
    low_mask,
    low_table,
    interp,
    shift_angle,
    par_source,
    par_index,
    par_mask,
    par_table,
):
    box_dev = patterns.shape[1]
    blocks_each = box_dev // 8
    directions = interp.shape[1]
    illums = patterns.shape[3]
    groups = lax.axis_size("box")
    listed = owner_block.shape[0]
    cosine = jnp.cos(shift_angle)[None, :, :, None]
    sine = jnp.sin(shift_angle)[None, :, :, None]
    operator = low_table[:, low_index] * low_mask[None, :, :, None].astype(jnp.bfloat16)
    pieces = []
    for listed_step in range(listed):
        owner = owner_block[listed_step]
        local_block = lax.dynamic_slice_in_dim(patterns, owner % blocks_each * 8, 8, 1)
        pieces.append(broadcast(local_block, "box", owner // blocks_each))
    far_boxes = jnp.concatenate(pieces, axis=1)
    near = complex_apply(operator, jnp.concatenate([patterns, far_boxes], axis=1))
    lifted = jnp.einsum("cbkr,kq->cbqr", patterns, interp, preferred_element_type=jnp.float32)
    lifted = lifted.reshape(2, blocks_each, 8, directions, illums)
    real_part = jnp.sum(cosine * lifted[0] - sine * lifted[1], axis=1)
    imaginary = jnp.sum(cosine * lifted[1] + sine * lifted[0], axis=1)
    parent_local = jnp.stack([real_part, imaginary]).astype(jnp.bfloat16)
    parents_total = par_source.shape[0]
    dir_local = directions // groups
    dir_start = lax.axis_index("box") * dir_local
    table_slice = lax.dynamic_slice_in_dim(par_table, dir_start, dir_local, 2)
    rows = table_slice[:, par_index]
    selector = (
        (par_source[:, :, None] == jnp.arange(parents_total, dtype=jnp.int32)[None, None, :])
        & (par_mask[:, :, None] > 0)
    ).astype(jnp.bfloat16)
    coupling = jnp.einsum(
        "pjs,cpjq->cqps", selector, rows, preferred_element_type=jnp.float32
    ).astype(jnp.bfloat16)
    block = lax.all_to_all(parent_local, "box", split_axis=2, concat_axis=1, tiled=True)

    def single(left, right):
        return jnp.einsum("qps,sqr->pqr", left, right, preferred_element_type=jnp.float32)

    real_out = single(coupling[0], block[0]) - single(coupling[1], block[1])
    imag_out = single(coupling[0], block[1]) + single(coupling[1], block[0])
    result = jnp.stack([real_out, imag_out]).astype(jnp.bfloat16)
    translated = lax.all_to_all(result, "box", split_axis=1, concat_axis=2, tiled=True)
    wide = translated.astype(jnp.float32)[:, :, None]
    real_down = cosine * wide[0] + sine * wide[1]
    imag_down = cosine * wide[1] - sine * wide[0]
    phased = (
        jnp.stack([real_down, imag_down])
        .astype(jnp.bfloat16)
        .reshape(2, box_dev, directions, illums)
    )
    down = jnp.einsum("cbqr,kq->cbkr", phased, interp, preferred_element_type=jnp.float32)
    return near + down


def solution(mesh):
    placed = (
        P(None, "box", None, "illum"),
        P(),
        P("box", None),
        P("box", None),
        P(),
        P(),
        P(),
        P(),
        P(),
        P(),
        P(),
    )
    return jax.shard_map(
        shards, mesh=mesh, in_specs=placed, out_specs=P(None, "box", None, "illum"), check_vma=False
    )
```

profile of v0, /device:TPU:1, one launch (start us, length us, event | category | flops | bytes accessed | tf_op | source)
XLA Modules:
  0.0 195.4 jit_solution(7571695900669596323)
XLA Ops:
  6.5 0.9 fusion.40
  7.4 2.6 %convolution_bitcast_fusion = f32[2,16,512,128]{3,2,1,0:T(8,128)S(1)} fusion(bf16[2,16,128,128]{3,2,1,0:T(8,128)(2,1)} %param.11, bf16[128,512]{1,0:T(8,128)(2,1)} %param.16), kind=kOutput, calls=%fused_computation.16 | convolution fusion | flops 536870912 | bytes 9568256 | tf_op jit(solution)/shard_map/cbkr,kq->cbqr/dot_general | solution.py:51
  10.0 0.9 fusion.36
  10.9 1.6 subtract_reduce_fusion
  12.6 0.0 copy-start.12
  12.6 0.1 pad_maximum_fusion
  12.7 1.3 copy.132
  14.0 8.6 %all-to-all-start = ((bf16[2,2,512,128]{3,1,0,2:T(2,128)(2,1)}), bf16[2,2,512,128]{3,1,0,2:T(2,128)(2,1)}, u32[]{:S(2)}, u32[]{:S(2)}) async-start(bf16[2,2,512,128]{3,1,0,2:T(2,128)(2,1)} %copy.132), calls=%async_computation | async-start | bytes 1048576 | tf_op jit(solution)/shard_map/all_to_all | solution.py:68
  22.7 0.7 fusion.41
  33.5 0.1 copy.135
  33.6 0.1 reshape.109
  33.7 0.1 reshape.101
  33.8 0.2 constant_dynamic-slice_fusion
  34.0 0.6 pad_clamp_fusion
  34.6 3.7 %gather_fusion.1 = bf16[1024,2,16]{2,1,0:T(2,128)(2,1)S(1)} fusion(bf16[2,316,16]{2,0,1:T(2,128)(2,1)S(1)} %constant_dynamic-slice_fusion, s32[1024]{0:T(1024)S(1)} %get-tuple-element.34), kind=kCustom, calls=%fused_computation.1 | custom fusion | bytes 135168 | tf_op jit(solution)/shard_map/gather | solution.py:60
  38.3 0.4 copy.136
  38.8 0.1 copy.137
  38.9 0.1 copy.138
  39.1 0.5 fusion.16
  39.6 0.7 slice_bitcast_fusion.20
  40.3 3.0 %fusion.38 = (bf16[2,16,128,128]{3,1,2,0:T(8,128)(2,1)}, bf16[2,48,128,128]{3,1,2,0:T(8,128)(2,1)S(1)}) fusion(bf16[2,16,128,128]{3,2,1,0:T(8,128)(2,1)} %param.11), kind=kLoop, calls=%fused_computation.80 | loop fusion | bytes 3145728 | tf_op args[0]
  43.3 1.2 copy.133
  44.5 0.3 copy.134
  44.8 0.3 copy.140
  45.1 0.2 fusion.29
  45.3 0.2 fusion.31
  45.5 0.2 fusion.20
  45.7 0.2 fusion.19
  46.0 0.1 pad_maximum_fusion.1
  46.0 1.1 copy.144
  47.2 7.4 %all-to-all-start.1 = ((bf16[2,64,16,128]{3,2,0,1:T(8,128)(2,1)}), bf16[2,64,16,128]{3,2,0,1:T(8,128)(2,1)}, u32[]{:S(2)}, u32[]{:S(2)}) async-start(bf16[2,64,16,128]{3,2,0,1:T(8,128)(2,1)} %copy.144), calls=%async_computation.1 | async-start | bytes 1048576 | tf_op jit(solution)/shard_map/all_to_all | solution.py:76
  54.6 0.2 all-reduce.3.cloned.1.call-start
  54.8 3.3 %dynamic-slice_select_fusion = (bf16[2,8,128,128]{3,1,2,0:T(8,128)(2,1)}, bf16[2,8,128,128]{3,1,2,0:T(8,128)(2,1)}, bf16[2,8,128,128]{3,1,2,0:T(8,128)(2,1)}, bf16[2,8,128,128]{3,1,2,0:T(8,128)(2,1)}) fusion(bf16[2,16,128,128]{3,1,2,0:T(8,128)(2,1)} %get-tuple-element.21, s32[]{:T(128)S(6)} %select_n.97, pred[]{:T(512)S(6)} %eq.33, s32[]{:T(128)S(6)} %select_n.92, ...), kind=kLoop, calls=%fused_computation.44 | loop fusion | flops 1048576 | bytes 4194324 | tf_op jit(solution)/shard_map/jit(_where)/select_n | solution.py:9
  58.2 0.0 all-reduce.3.cloned.1.call-update
  58.2 2.8 %gather_fusion = bf16[768,2,128]{2,1,0:T(2,128)(2,1)S(1)} fusion(bf16[2,316,128]{2,0,1:T(2,128)(2,1)} %param.15, s32[1024]{0:T(1024)} %get-tuple-element.33), kind=kCustom, calls=%fused_computation | custom fusion | bytes 789504 | tf_op jit(solution)/shard_map/gather | solution.py:43
  61.0 1.4 copy.130
  62.4 0.7 convert_element_type.25
  63.1 0.7 broadcast_bitcast_fusion
  63.9 2.3 %multiply_bitcast_fusion = bf16[2,16,48,128]{2,1,3,0:T(8,128)(2,1)} fusion(bf16[16,48,2,128]{1,0,3,2:T(8,128)(2,1)} %copy.130, bf16[16,48]{1,0:T(8,128)(2,1)S(1)} %convert_element_type.25), kind=kLoop, calls=%fused_computation.37 | loop fusion | flops 196608 | bytes 787968 | tf_op jit(solution)/shard_map/mul | solution.py:43
  66.1 0.1 all-to-all-done.1
  66.3 1.1 copy.145
  67.4 0.1 convert_bitcast_fusion
  67.5 0.9 fusion.37
  68.4 0.8 copy.146
  69.2 2.0 %copy.147 = f32[2,512,128]{1,2,0:T(8,128)} copy(f32[2,512,128]{2,1,0:T(8,128)} %bitcast.133) | data formatting | bytes 1048576 | tf_op jit(solution)/shard_map/mul | solution.py:78
  71.2 1.9 copy.148
  73.1 2.0 %copy.149 = f32[2,512,128]{1,2,0:T(8,128)} copy(f32[2,512,128]{2,1,0:T(8,128)} %bitcast.134) | data formatting | bytes 1048576 | tf_op jit(solution)/shard_map/mul | solution.py:78
  75.2 1.6 mul.176
  76.8 0.5 mul.183
  77.4 1.6 fusion.1
  79.0 2.6 %fusion.4 = f32[2,16,128,128]{3,2,1,0:T(8,128)} fusion(bf16[1,16,512,128]{2,3,1,0:T(8,128)(2,1)S(1)} %get-tuple-element.12, bf16[1,16,512,128]{2,3,1,0:T(8,128)(2,1)S(1)} %get-tuple-element.11, bf16[128,512]{1,0:T(8,128)(2,1)S(1)} %copy-done.8), kind=kOutput, calls=%fused_computation.10 | convolution fusion | flops 538968064 | bytes 6422528 | tf_op jit(solution)/shard_map/cbqr,kq->cbkr/dot_general | solution.py:85
  81.6 3.0 %copy.150 = f32[2,16,128,128]{2,1,3,0:T(8,128)} copy(f32[2,16,128,128]{3,2,1,0:T(8,128)} %fusion.4) | data formatting | bytes 4194304 | tf_op jit(solution)/shard_map/cbqr,kq->cbkr/dot_general | solution.py:85
  84.6 94.7 %all-reduce.3.cloned.1.call-done = (bf16[2,8,128,128]{3,1,2,0:T(8,128)(2,1)}, bf16[2,8,128,128]{3,1,2,0:T(8,128)(2,1)}, bf16[2,8,128,128]{3,1,2,0:T(8,128)(2,1)}, bf16[2,8,128,128]{3,1,2,0:T(8,128)(2,1)}) async-done(((bf16[2,8,128,128]{3,1,2,0:T(8,128)(2,1)}, bf16[2,8,128,128]{3,1,2,0:T(8,128)(2,1)}, bf16[2,8,128,128]{3,1,2,0:T(8,128)(2,1)}, bf16[2,8,128,128]{3,1,2,0:T(8,128)(2,1)}), ...) | async-done | bytes 2097168 | tf_op jit(solution)/shard_map/psum | solution.py:9
  179.3 1.3 constant_dynamic-update-slice_fusion.3
  180.6 1.2 constant_dynamic-update-slice_fusion.2
  181.7 1.2 constant_dynamic-update-slice_fusion.1
  182.9 0.1 constant_dynamic-update-slice_fusion
  183.1 0.5 fusion.8
  183.6 0.5 fusion.9
  184.1 0.6 fusion.15
  184.7 0.5 fusion.13
  185.3 1.0 copy-done.3
  186.3 0.3 maximum_add_fusion
  186.6 1.9 copy.151
  (31 shorter events, 0.1 us)
Async XLA Ops:
  6.5 27.2 %copy-start = (bf16[2,316,512]{2,0,1:T(2,128)(2,1)S(1)}, bf16[2,316,512]{2,0,1:T(2,128)(2,1)}, u32[]{:S(2)}) copy-start(bf16[2,316,512]{2,0,1:T(2,128)(2,1)} %param.21) | copy-start | bytes 1941508
  7.4 3.5 %copy-start.7 = (f32[8,512]{1,0:T(8,128)}, f32[8,512]{1,0:T(8,128)S(1)}, u32[]{:S(2)}) copy-start(f32[8,512]{1,0:T(8,128)S(1)} %get-tuple-element.28) | copy-start | bytes 49156
  12.5 10.1 %copy-start.13 = (s32[4]{0:T(128)S(1)}, s32[4]{0:T(128)}, u32[]{:S(2)}) copy-start(s32[4]{0:T(128)} %param.12) | copy-start | bytes 52
  12.6 21.0 %copy-start.11 = (s32[64,16]{0,1:T(8,128)S(1)}, s32[64,16]{0,1:T(8,128)}, u32[]{:S(2)}) copy-start(s32[64,16]{0,1:T(8,128)} %param.19) | copy-start | bytes 12292
  12.6 21.1 %copy-start.12 = (s32[16,48]{1,0:T(8,128)S(1)}, s32[16,48]{1,0:T(8,128)}, u32[]{:S(2)}) copy-start(s32[16,48]{1,0:T(8,128)} %param.13) | copy-start | bytes 9220
  12.6 26.2 %copy-start.9 = (s32[64,16]{0,1:T(8,128)S(1)}, s32[64,16]{0,1:T(8,128)}, u32[]{:S(2)}) copy-start(s32[64,16]{0,1:T(8,128)} %param.18) | copy-start | bytes 12292
  12.6 26.3 %copy-start.10 = (s32[64,16]{0,1:T(8,128)S(1)}, s32[64,16]{0,1:T(8,128)}, u32[]{:S(2)}) copy-start(s32[64,16]{0,1:T(8,128)} %param.20) | copy-start | bytes 12292
  14.0 29.3 %all-to-all-start = ((bf16[2,2,512,128]{3,1,0,2:T(2,128)(2,1)}), bf16[2,2,512,128]{3,1,0,2:T(2,128)(2,1)}, u32[]{:S(2)}, u32[]{:S(2)}) async-start(bf16[2,2,512,128]{3,1,0,2:T(2,128)(2,1)} %copy.132), calls=%async_computation | async-start | bytes 1048576 | tf_op jit(solution)/shard_map/all_to_all | solution.py:68
  43.3 1.8 copy-start.4
  47.2 19.1 %all-to-all-start.1 = ((bf16[2,64,16,128]{3,2,0,1:T(8,128)(2,1)}), bf16[2,64,16,128]{3,2,0,1:T(8,128)(2,1)}, u32[]{:S(2)}, u32[]{:S(2)}) async-start(bf16[2,64,16,128]{3,2,0,1:T(8,128)(2,1)} %copy.144), calls=%async_computation.1 | async-start | bytes 1048576 | tf_op jit(solution)/shard_map/all_to_all | solution.py:76
  54.6 124.7 %all-reduce.3.cloned.1.call-start = ((), (), s32[]{:S(2)}) async-start(), calls=%async_computation.2 | async-start | bytes 4194304 | tf_op jit(solution)/shard_map/psum | solution.py:9
  75.2 1.6 copy-start.5
  77.4 1.6 copy-start.8
  179.3 3.6 %copy-start.6 = (bf16[2,8,128,128]{3,1,2,0:T(8,128)(2,1)S(1)}, bf16[2,8,128,128]{3,1,2,0:T(8,128)(2,1)}, u32[]{:S(2)}) copy-start(bf16[2,8,128,128]{3,1,2,0:T(8,128)(2,1)} %get-tuple-element.10) | copy-start | bytes 1572868
  179.3 3.8 %copy-start.2 = (bf16[2,16,48,128]{2,1,3,0:T(8,128)(2,1)S(1)}, bf16[2,16,48,128]{2,1,3,0:T(8,128)(2,1)}, u32[]{:S(2)}) copy-start(bf16[2,16,48,128]{2,1,3,0:T(8,128)(2,1)} %multiply_bitcast_fusion) | copy-start | bytes 1179652
  184.7 1.6 copy-start.3
  186.3 2.2 %copy-start.1 = (bf16[2,316,512]{2,0,1:T(2,128)(2,1)S(1)}, bf16[2,316,512]{2,0,1:T(2,128)(2,1)}, u32[]{:S(2)}) copy-start(bf16[2,316,512]{2,0,1:T(2,128)(2,1)} %param.21) | copy-start | bytes 1941508
Sparse Core Ops, SparseCore 0:
  58.9 120.3 all-reduce.2
where the time goes:
time: 196 us; the launch traced here: 195 us
  waiting for transfers between devices  94.8 us (48%)
  local copies, waits for them, and re-layouts  40.8 us (21%)
  between operations  24.1 us (12%)
  starting transfers between devices  16.3 us (8%)
  other arithmetic  10.7 us (5%)
  matrix products  8.65 us (4%)
    psum x1, waiting for transfers between devices, broadcast(): return lax.psum(jnp.where(mine, x, jnp.zeros_like(x)), axis)  94.7 us
    all_to_all x1, starting transfers between devices, shards(): lax.all_to_all(parent_local, 'box', split_axis=2, concat_axis=1, tiled=True)  8.64 us
    unnamed x33, local copies, waits for them, and re-layouts  7.81 us
    all_to_all x1, starting transfers between devices, shards(): lax.all_to_all(result, 'box', split_axis=1, concat_axis=2, tiled=True)  7.44 us
    mul x4, local copies, waits for them, and re-layouts, shards(): real_down = cosine * wide[0] + sine * wide[1]  6.24 us
    gather x2, local copies, waits for them, and re-layouts, shards(): low_table[:, low_index] * low_mask[None, :, :, None].astype(jnp.bfloat16)  4.23 us
    gather x2, local copies, waits for them, and re-layouts, shards(): rows = table_slice[:, par_index]  4.11 us
  transfers between devices with their start and end apart: 3, of which 2 were waited for; matrix products, arithmetic and copies ran while one was open for 20% of the time, Pallas kernels for 0%

commit v1 on v0

v1 whole, which is shorter than its diff:
```python
import jax
import jax.numpy as jnp
from jax import lax
from jax.experimental import pallas as pl
from jax.experimental.pallas import tpu as pltpu
from jax.sharding import PartitionSpec as P

F32 = jnp.float32
BF16 = jnp.bfloat16
LANES = 128
LIMIT = 48 * 1024 * 1024
DEV = 32
BOX = 16
K = 128
Q = 512
R = 128
QS = Q // DEV
KS = K // DEV
NPAD = 384
FAR = 32
L_ROWS = 4 * QS
P_ROWS = 2 * KS * 8
T_ROWS = 2 * BOX
SEND1 = L_ROWS + P_ROWS + T_ROWS
N_ROWS = 2 * KS * BOX
SEND2 = L_ROWS + N_ROWS


def iota(shape, dim):
    return lax.broadcasted_iota(jnp.int32, shape, dim)


def pick(row, index, chunk):
    total = None
    for part in range(NPAD // LANES):
        source = jnp.broadcast_to(row(part), index.shape)
        got = jnp.take_along_axis(source, index, axis=1, mode="promise_in_bounds")
        total = got if total is None else jnp.where(chunk == part, got, total)
    return total


def split(out_ref, c, rows):
    for part in range(NPAD // LANES):
        out_ref[c, part] = rows[:, part * LANES : (part + 1) * LANES]


def transpose_table(table_ref, out_ref):
    count = table_ref.shape[1]
    for part in range(2):
        wide = table_ref[part].astype(F32)
        wide = jnp.concatenate([wide, jnp.zeros((NPAD - count, wide.shape[1]), F32)], axis=0)
        split(out_ref, part, jnp.transpose(wide))


def first_parity(owner, device):
    result = jnp.int32(0)
    for step in reversed(range(owner.shape[0])):
        value = owner[step]
        result = jnp.where((value >> 1) == device, value & 1, result)
    return result


def up_kernel(
    owner, patterns, index, mask, table, interp, angle, send, extra, flag,
    weights, fields, wide, table_t, spread,
):
    me = lax.axis_index("box")
    interp_t = jnp.transpose(interp[...].astype(F32))
    cosine = jnp.transpose(jnp.cos(angle[...]))
    sine = jnp.transpose(jnp.sin(angle[...]))
    for b in range(8):
        rows = 2 * b * K
        weights[:, rows : rows + K] = (interp_t * cosine[:, b : b + 1]).astype(BF16)
        weights[:, rows + K : rows + 2 * K] = (interp_t * sine[:, b : b + 1]).astype(BF16)
        for p in range(2):
            real, imag = patterns[0, 8 * p + b], patterns[1, 8 * p + b]
            fields[rows : rows + K, p * R : (p + 1) * R] = real
            fields[rows + K : rows + 2 * K, p * R : (p + 1) * R] = -imag
            fields[rows : rows + K, (2 + p) * R : (3 + p) * R] = imag
            fields[rows + K : rows + 2 * K, (2 + p) * R : (3 + p) * R] = real
    tile = 128
    for t in range(Q // tile):
        total = jnp.dot(
            weights[t * tile : (t + 1) * tile, :], fields[...], preferred_element_type=F32
        ).astype(BF16)
        ways = tile // QS
        for cp in range(4):
            send[t * ways : (t + 1) * ways, cp * QS : (cp + 1) * QS, :] = total[
                :, cp * R : (cp + 1) * R
            ].reshape(ways, QS, R)

    for c in range(2):
        for b in range(BOX):
            wide[c, b * K : (b + 1) * K, :] = patterns[c, b].astype(F32)
    first = first_parity(owner, me)

    def cut(out, base, parity):
        def one(d, _):
            for c in range(2):
                for half in range(KS // 2):
                    pieces = [
                        wide[c, pl.ds(parity * (8 * K) + d * KS + 2 * half + k, 8, stride=K), :]
                        for k in range(2)
                    ]
                    out[d, base + c * KS * 8 + half * 16 : base + c * KS * 8 + (half + 1) * 16, :] = (
                        jnp.concatenate(pieces, axis=0).astype(BF16)
                    )
            return 0

        lax.fori_loop(0, DEV, one, 0)

    cut(send, L_ROWS, first)
    twice = jnp.int32(0)
    for i in range(owner.shape[0]):
        for j in range(i):
            same = (owner[i] >> 1) == (owner[j] >> 1)
            twice = jnp.where(same & (owner[i] != owner[j]), 1, twice)
    flag[0] = twice

    @pl.when(twice > 0)
    def _():
        cut(extra, 0, 1 - first)

    transpose_table(table, table_t)
    near_count = BOX
    spread[:, 0 : index.shape[1]] = jnp.where(mask[...] > 0, index[...], NPAD - 1)
    lane = iota((BOX, LANES), 1)
    code = jnp.take_along_axis(
        spread[...], near_count + (lane & (FAR - 1)), axis=1, mode="promise_in_bounds"
    )
    low, chunk = code & (LANES - 1), code >> 7

    def operators(d, _):
        for c in range(2):
            total = jnp.zeros((BOX, LANES), F32)
            for k in range(KS):
                got = pick(
                    lambda part: table_t[c, part, pl.ds(d * KS + k, 1), :], low, chunk
                )
                total = jnp.where((lane >> 5) == k, got, total)
            at = L_ROWS + P_ROWS + c * BOX
            send[d, at : at + BOX, :] = total.astype(BF16)
        return 0

    lax.fori_loop(0, DEV, operators, 0)


def side_kernel(
    patterns, index, mask, table, par_source, par_index, par_mask, par_table, near, coupling,
    wide, table_t, par_t, spread, left, right,
):
    me = lax.axis_index("box")
    for c in range(2):
        for b in range(BOX):
            wide[c, b * K : (b + 1) * K, :] = patterns[c, b].astype(F32)
    transpose_table(table, table_t)
    spread[:, 0 : index.shape[1]] = jnp.where(mask[...] > 0, index[...], NPAD - 1)
    lane = iota((BOX, LANES), 1)
    code = jnp.take_along_axis(spread[...], lane & (BOX - 1), axis=1, mode="promise_in_bounds")
    low, chunk = code & (LANES - 1), code >> 7
    imaginary = ((lane >> 4) & 1) == 1
    left[...] = jnp.zeros_like(left)

    def group(g, _):
        for kk in range(8):
            k = g * 8 + kk
            got = [
                pick(lambda part: table_t[c, part, pl.ds(k, 1), :], low, chunk)
                for c in range(2)
            ]
            value = jnp.where(imaginary, got[1], got[0])
            value = jnp.where((lane >> 5) == kk % 4, value, 0.0).astype(BF16)
            at = kk // 4 * LANES
            left[kk * BOX : (kk + 1) * BOX, at : at + LANES] = value
            real = wide[0, pl.ds(k, BOX, stride=K), :]
            imag = wide[1, pl.ds(k, BOX, stride=K), :]
            row = kk * 2 * BOX
            right[row : row + BOX, 0:R] = real.astype(BF16)
            right[row : row + BOX, R : 2 * R] = imag.astype(BF16)
            right[row + BOX : row + 2 * BOX, 0:R] = (-imag).astype(BF16)
            right[row + BOX : row + 2 * BOX, R : 2 * R] = real.astype(BF16)
        total = jnp.dot(left[...], right[...], preferred_element_type=F32)
        for kk in range(8):
            for c in range(2):
                near[c, pl.ds(g * 8 + kk, BOX, stride=K), :] = total[
                    kk * BOX : (kk + 1) * BOX, c * R : (c + 1) * R
                ]
        return 0

    lax.fori_loop(0, K // 8, group, 0)

    chosen = (iota((QS, Q), 1) == me * QS + iota((QS, Q), 0)).astype(BF16)
    count = par_table.shape[1]
    for c in range(2):
        rows = lax.dot_general(
            chosen, par_table[c], (((1,), (1,)), ((), ())), preferred_element_type=F32
        )
        split(par_t, c, jnp.concatenate([rows, jnp.zeros((QS, NPAD - count), F32)], axis=1))
    parents = 2 * DEV
    lanes = iota((parents, LANES), 1)
    source_here = (lanes & (DEV - 1)) * 2 + ((lanes >> 5) & 1)

    def halves(ref):
        return jnp.concatenate([ref[pl.ds(p, DEV, stride=2), :] for p in range(2)], axis=0)

    source, which, used = halves(par_source), halves(par_index), halves(par_mask)
    which = jnp.where(used > 0, which, NPAD - 1)
    table_at = jnp.full((parents, LANES), NPAD - 1, jnp.int32)
    for j in range(source.shape[1]):
        table_at = jnp.where(source[:, j : j + 1] == source_here, which[:, j : j + 1], table_at)
    par_low, par_chunk = table_at & (LANES - 1), table_at >> 7
    par_imaginary = lanes >= parents

    def one_q(q, _):
        got = [
            pick(lambda part: par_t[c, part, pl.ds(q, 1), :], par_low, par_chunk)
            for c in range(2)
        ]
        coupling[q] = jnp.where(par_imaginary, got[1], got[0]).astype(BF16)
        return 0

    lax.fori_loop(0, QS, one_q, 0)


def middle_kernel(owner, received, extra, coupling, send, far, fields, lifted, right, moved):
    for s in range(owner.shape[0]):
        block = owner[s]
        device = block >> 1
        second = (block & 1) != first_parity(owner, device)

        def place(ref, base):
            for c in range(2):
                for half in range(KS // 2):
                    at = base + c * KS * 8 + half * 16
                    piece = ref[device, at : at + 16, :].astype(F32)
                    for k in range(2):
                        row = (2 * half + k) * FAR + s * 8
                        fields[c, row : row + 8, :] = piece[8 * k : 8 * k + 8]

        @pl.when(jnp.logical_not(second))
        def _():
            place(received, L_ROWS)

        @pl.when(second)
        def _():
            place(extra, 0)

    at = L_ROWS + P_ROWS
    operators = jnp.concatenate(
        [received[:, at + c * BOX : at + (c + 1) * BOX, :].reshape(DEV * BOX, LANES) for c in range(2)],
        axis=1,
    )
    far[...] = jnp.zeros_like(far)
    for k in range(KS):
        rows = slice(k * FAR, (k + 1) * FAR)
        under = slice(LANES + k * FAR, LANES + (k + 1) * FAR)
        real, imag = fields[0, rows, :], fields[1, rows, :]
        far[k, rows, 0:R] = real.astype(BF16)
        far[k, rows, R : 2 * R] = imag.astype(BF16)
        far[k, under, 0:R] = (-imag).astype(BF16)
        far[k, under, R : 2 * R] = real.astype(BF16)
    for k in range(KS):
        total = jnp.dot(operators, far[k], preferred_element_type=F32).astype(BF16)
        for c in range(2):
            row = L_ROWS + (c * KS + k) * BOX
            send[:, row : row + BOX, :] = total[:, c * R : (c + 1) * R].reshape(DEV, BOX, R)

    size = DEV * QS
    for cp in range(4):
        lifted[cp * size : (cp + 1) * size, :] = (
            received[:, cp * QS : (cp + 1) * QS, :].reshape(size, R).astype(F32)
        )

    def one_q(q, _):
        parts = [lifted[pl.ds(cp * size + q, DEV, stride=QS), :] for cp in range(4)]
        real = jnp.concatenate(parts[:2], axis=0)
        imag = jnp.concatenate(parts[2:], axis=0)
        right[0 : 2 * DEV, 0:R] = real.astype(BF16)
        right[0 : 2 * DEV, R : 2 * R] = imag.astype(BF16)
        right[2 * DEV : 4 * DEV, 0:R] = (-imag).astype(BF16)
        right[2 * DEV : 4 * DEV, R : 2 * R] = real.astype(BF16)
        total = jnp.dot(coupling[q], right[...], preferred_element_type=F32)
        for c in range(2):
            for p in range(2):
                moved[pl.ds((2 * c + p) * size + q, DEV, stride=QS), :] = total[
                    p * DEV : (p + 1) * DEV, c * R : (c + 1) * R
                ]
        return 0

    lax.fori_loop(0, QS, one_q, 0)
    for cp in range(4):
        send[:, cp * QS : (cp + 1) * QS, :] = (
            moved[cp * size : (cp + 1) * size, :].reshape(DEV, QS, R).astype(BF16)
        )


def down_kernel(received, near, interp, angle, out, fields, far, cosine, sine):
    b = pl.program_id(0)

    @pl.when(b == 0)
    def _():
        cosine[...] = jnp.cos(angle[...])
        sine[...] = jnp.sin(angle[...])
        for p in range(2):
            real = received[:, p * QS : (p + 1) * QS, :].reshape(Q, R)
            imag = received[:, (2 + p) * QS : (3 + p) * QS, :].reshape(Q, R)
            fields[0:Q, p * R : (p + 1) * R] = real
            fields[Q : 2 * Q, p * R : (p + 1) * R] = imag
            fields[0:Q, (2 + p) * R : (3 + p) * R] = imag
            fields[Q : 2 * Q, (2 + p) * R : (3 + p) * R] = -real
        for c in range(2):
            row = L_ROWS + c * KS * BOX
            far[c] = received[:, row : row + KS * BOX, :].reshape(K * BOX, R).astype(F32)

    wide = interp[...].astype(F32)
    weights = jnp.concatenate(
        [
            (wide * cosine[pl.ds(b, 1), :]).astype(BF16),
            (wide * sine[pl.ds(b, 1), :]).astype(BF16),
        ],
        axis=1,
    )
    total = jnp.dot(weights, fields[...], preferred_element_type=F32)
    for c in range(2):
        for p in range(2):
            there = far[c, pl.ds(8 * p + b, K, stride=BOX), :]
            out[c, p, 0] = total[:, (2 * c + p) * R : (2 * c + p + 1) * R] + near[c, p, 0] + there


def in_vmem(count):
    return [pl.BlockSpec(memory_space=pltpu.VMEM)] * count


SCALARS = pl.BlockSpec(memory_space=pltpu.SMEM)


def params():
    return pltpu.CompilerParams(vmem_limit_bytes=LIMIT)


def shards(
    patterns,
    owner_block,
    low_index,
    low_mask,
    low_table,
    interp,
    shift_angle,
    par_source,
    par_index,
    par_mask,
    par_table,
):
    assert patterns.shape == (2, BOX, K, R) and interp.shape == (K, Q)
    assert lax.axis_size("box") == DEV and low_index.shape == (BOX, BOX + FAR)
    send, extra, flag = pl.pallas_call(
        up_kernel,
        out_shape=(
            jax.ShapeDtypeStruct((DEV, SEND1, R), BF16),
            jax.ShapeDtypeStruct((DEV, P_ROWS, R), BF16),
            jax.ShapeDtypeStruct((1,), jnp.int32),
        ),
        in_specs=[SCALARS] + in_vmem(6),
        out_specs=(*in_vmem(2), SCALARS),
        scratch_shapes=[
            pltpu.VMEM((Q, 16 * K), BF16),
            pltpu.VMEM((16 * K, 4 * R), BF16),
            pltpu.VMEM((2, BOX * K, R), F32),
            pltpu.VMEM((2, NPAD // LANES, K, LANES), F32),
            pltpu.VMEM((BOX, LANES), jnp.int32),
        ],
        compiler_params=params(),
        cost_estimate=pl.CostEstimate(
            flops=1200000000, bytes_accessed=4000000, transcendentals=8192
        ),
        name="up",
    )(owner_block, patterns, low_index, low_mask, low_table, interp, shift_angle)

    received = lax.all_to_all(send, "box", split_axis=0, concat_axis=0, tiled=True)

    near, coupling = pl.pallas_call(
        side_kernel,
        out_shape=(
            jax.ShapeDtypeStruct((2, BOX * K, R), F32),
            jax.ShapeDtypeStruct((QS, 2 * DEV, LANES), BF16),
        ),
        in_specs=in_vmem(8),
        out_specs=tuple(in_vmem(2)),
        scratch_shapes=[
            pltpu.VMEM((2, BOX * K, R), F32),
            pltpu.VMEM((2, NPAD // LANES, K, LANES), F32),
            pltpu.VMEM((2, NPAD // LANES, QS, LANES), F32),
            pltpu.VMEM((BOX, LANES), jnp.int32),
            pltpu.VMEM((8 * BOX, 2 * LANES), BF16),
            pltpu.VMEM((2 * LANES, 2 * R), BF16),
        ],
        compiler_params=params(),
        cost_estimate=pl.CostEstimate(
            flops=4000000000, bytes_accessed=12000000, transcendentals=0
        ),
        name="side",
    )(patterns, low_index, low_mask, low_table, par_source, par_index, par_mask, par_table)

    extra = lax.cond(
        flag[0] > 0,
        lambda x: lax.all_to_all(x, "box", split_axis=0, concat_axis=0, tiled=True),
        lambda x: x,
        extra,
    )

    size = DEV * QS
    send = pl.pallas_call(
        middle_kernel,
        out_shape=jax.ShapeDtypeStruct((DEV, SEND2, R), BF16),
        in_specs=[SCALARS] + in_vmem(3),
        out_specs=in_vmem(1)[0],
        scratch_shapes=[
            pltpu.VMEM((KS, 2 * LANES, 2 * R), BF16),
            pltpu.VMEM((2, KS * FAR, R), F32),
            pltpu.VMEM((4 * size, R), F32),
            pltpu.VMEM((4 * DEV, 2 * R), BF16),
            pltpu.VMEM((4 * size, R), F32),
        ],
        compiler_params=params(),
        cost_estimate=pl.CostEstimate(
            flops=800000000, bytes_accessed=4000000, transcendentals=0
        ),
        name="middle",
    )(owner_block, received, extra, coupling)

    received = lax.all_to_all(send, "box", split_axis=0, concat_axis=0, tiled=True)

    block = pl.BlockSpec((2, 2, 1, K, R), lambda b: (0, 0, b, 0, 0))
    whole = [
        pl.BlockSpec(shape, lambda b, n=len(shape): (0,) * n)
        for shape in ((DEV, SEND2, R), (K, Q), (8, Q))
    ]
    out = pl.pallas_call(
        down_kernel,
        grid=(8,),
        out_shape=jax.ShapeDtypeStruct((2, 2, 8, K, R), F32),
        in_specs=[whole[0], block, whole[1], whole[2]],
        out_specs=block,
        scratch_shapes=[
            pltpu.VMEM((2 * Q, 4 * R), BF16),
            pltpu.VMEM((2, K * BOX, R), F32),
            pltpu.VMEM((8, Q), F32),
            pltpu.VMEM((8, Q), F32),
        ],
        compiler_params=params(),
        cost_estimate=pl.CostEstimate(
            flops=1200000000, bytes_accessed=6000000, transcendentals=8192
        ),
        name="down",
    )(received, near.reshape(2, 2, 8, K, R), interp, shift_angle)
    return out.reshape(2, BOX, K, R)


def solution(mesh):
    placed = (
        P(None, "box", None, "illum"),
        P(),
        P("box", None),
        P("box", None),
        P(),
        P(),
        P(),
        P(),
        P(),
        P(),
        P(),
    )
    return jax.shard_map(
        shards, mesh=mesh, in_specs=placed, out_specs=P(None, "box", None, "illum"), check_vma=False
    )
```

time: 196 us -> 82.2 us (0.42)
  waiting for transfers between devices: 94.8 us -> 8.74 us
  local copies, waits for them, and re-layouts: 40.8 us -> 10.7 us
  blocking collectives: 0 us -> 26.7 us
  Pallas kernels: 0 us -> 26 us
  between operations: 24.1 us -> 0.89 us
  other arithmetic: 10.7 us -> 0 us
  matrix products: 8.65 us -> 0 us
  starting transfers between devices: 16.3 us -> 8.59 us
    psum x1 -> x0, waiting for transfers between devices: 94.7 us -> none  [broadcast(): return lax.psum(jnp.where(mine, x, jnp.zeros_like(x)), axis)]
    all_to_all x0 -> x1, blocking collectives: none -> 26.7 us  [shards(): lax.all_to_all(send, 'box', split_axis=0, concat_axis=0, tiled=True)]
    pallas_call x0 -> x4, Pallas kernels: none -> 26 us  [the longest x1 8.12 us: shards(): pl.pallas_call(up_kernel, out_shape=(jax.ShapeDtypeStruct((DEV, SEND1, R)...]
    dot_general x11 -> x0, matrix products: 8.65 us -> none  [the longest x1 2.58 us: shards(): jnp.einsum('cbkr,kq->cbqr', patterns, interp, preferred_element_type=jnp....]
    all_to_all x2 -> x1, waiting for transfers between devices: 0.14 us -> 8.74 us  [shards(): lax.all_to_all(send, 'box', split_axis=0, concat_axis=0, tiled=True)]
    gather x4 -> x0, local copies, waits for them, and re-layouts: 8.34 us -> none  [the longest x2 4.23 us: shards(): low_table[:, low_index] * low_mask[None, :, :, None].astype(jnp.bfloat16)]
    all_to_all x2 -> x1, starting transfers between devices: 16.1 us -> 8.59 us  [shards(): lax.all_to_all(send, 'box', split_axis=0, concat_axis=0, tiled=True)]
    mul x5 -> x0, local copies, waits for them, and re-layouts: 6.96 us -> none  [the longest x4 6.24 us: shards(): real_down = cosine * wide[0] + sine * wide[1]]
  transfers between devices with their start and end apart: 3 -> 1, of which waited for: 2 -> 1; matrix products, arithmetic and copies ran while one was open for 20% -> 0% of each run, Pallas kernels for 0% -> 10%
where the time goes in v1:
time: 82.2 us; the launch traced here: 81.6 us
  blocking collectives  26.7 us (32%)
  Pallas kernels  26 us (32%)
  local copies, waits for them, and re-layouts  10.7 us (13%)
  waiting for transfers between devices  8.74 us (11%)
  starting transfers between devices  8.59 us (10%)
  between operations  0.89 us (1%)
    all_to_all x1, blocking collectives, shards(): lax.all_to_all(send, 'box', split_axis=0, concat_axis=0, tiled=True)  26.7 us
    unnamed x47, local copies, waits for them, and re-layouts  10.7 us
    all_to_all x1, waiting for transfers between devices, shards(): lax.all_to_all(send, 'box', split_axis=0, concat_axis=0, tiled=True)  8.74 us
    all_to_all x1, starting transfers between devices, shards(): lax.all_to_all(send, 'box', split_axis=0, concat_axis=0, tiled=True)  8.59 us
    pallas_call x1, Pallas kernels, shards(): pl.pallas_call(up_kernel, out_shape=(jax.ShapeDtypeStruct((DEV, SEND1, R)...  8.12 us
    pallas_call x1, Pallas kernels, shards(): pl.pallas_call(side_kernel, out_shape=(jax.ShapeDtypeStruct((2, BOX * K,...  7.84 us
    pallas_call x1, Pallas kernels, shards(): pl.pallas_call(down_kernel, grid=(8,), out_shape=jax.ShapeDtypeStruct((2,...  5.05 us
    pallas_call x1, Pallas kernels, shards(): pl.pallas_call(middle_kernel, out_shape=jax.ShapeDtypeStruct((DEV, SEND2,...  4.97 us
  transfers between devices with their start and end apart: 1, of which 1 were waited for; matrix products, arithmetic and copies ran while one was open for 0% of the time, Pallas kernels for 10%

profile of v1, /device:TPU:1, one launch (start us, length us, event | category | flops | bytes accessed | tf_op | source)
XLA Modules:
  0.0 81.6 jit_solution(7549082925021742009)
XLA Ops:
  0.0 0.9 %copy.12.table = bf16[2,316,128]{2,1,0:T(8,128)(2,1)S(1)} copy(bf16[2,316,128]{2,0,1:T(2,128)(2,1)} %param.17) | data formatting | bytes 323584 | tf_op args[4]
  0.9 0.0 copy-start.4
  1.0 0.9 %copy-done.4 = bf16[128,512]{1,0:T(8,128)(2,1)S(1)} copy-done((bf16[128,512]{1,0:T(8,128)(2,1)S(1)}, bf16[128,512]{1,0:T(8,128)(2,1)}, u32[]{:S(2)}) %copy-start.4) | copy-done | bytes 131096
  1.8 0.0 copy-start.6
  1.9 0.7 copy-done.6
  2.6 0.0 copy-start.8
  2.6 0.7 copy-done.8
  3.2 0.0 copy-start.10
  3.2 1.2 %copy-done.10 = bf16[2,16,128,128]{3,2,1,0:T(8,128)(2,1)S(1)} copy-done((bf16[2,16,128,128]{3,2,1,0:T(8,128)(2,1)S(1)}, bf16[2,16,128,128]{3,2,1,0:T(8,128)(2,1)}, u32[]{:S(2)}) %copy-start.10) | copy-done | bytes 1048600
  4.4 0.0 copy-start.12
  4.4 0.7 copy-done.12
  5.1 0.0 copy-start.14
  5.1 0.7 copy-done.14
  5.8 0.0 copy-start.2
  5.8 8.1 %up.1 = (bf16[32,160,128]{2,1,0:T(8,128)(2,1)}, bf16[32,64,128]{2,1,0:T(8,128)(2,1)S(1)}, s32[1]{0:T(128)}) custom-call(s32[4]{0:T(128)S(1)} %copy-done.8, bf16[2,16,128,128]{3,2,1,0:T(8,128)(2,1)S(1)} %copy-done.10, s32[16,48]{1,0:T(8,128)S(1)} %copy-done.12, s32[16,48]{1,0:T(8,128)S(1)} %copy-done.14, bf16[2,316,128]{2,1,0:T(8,128)(2,1)S(1)} %copy.12.table, ...), custom_call_target="tpu_custom_call" | custom-call | flops 1200000000 | bytes 4000000 | tf_op jit(solution)/shard_map/up/pallas_call | solution.py:356
  14.0 0.0 copy-done.2
  14.7 0.0 copy-start.16
  14.7 0.0 copy-start.18
  14.7 0.0 copy-start.19
  14.7 0.0 copy-start.20
  14.7 0.0 copy-start.17
  14.7 0.0 copy-start.13
  14.8 0.0 copy-start.15
  14.8 0.7 copy-done.16
  15.5 8.6 %all-to-all-start.1 = ((bf16[32,160,128]{2,1,0:T(8,128)(2,1)}), bf16[32,160,128]{2,1,0:T(8,128)(2,1)S(1)}, u32[]{:S(2)}, u32[]{:S(2)}) async-start(bf16[32,160,128]{2,1,0:T(8,128)(2,1)} %get-tuple-element.15), calls=%async_computation.1 | async-start | bytes 2621440 | tf_op jit(solution)/shard_map/all_to_all | solution.py:379
  24.1 0.0 copy-done.18
  24.1 0.1 copy.14.par_source
  24.2 0.0 copy-done.19
  24.2 0.1 copy.15.par_index
  24.3 0.0 copy-done.20
  24.3 0.1 copy.16.par_mask
  24.4 0.0 copy-done.17
  24.4 0.1 copy.17.par_table
  24.4 0.0 copy-done.13
  24.4 0.0 copy-done.15
  24.5 0.0 copy-start.3
  24.5 0.9 %copy-done.3 = bf16[2,316,128]{2,1,0:T(8,128)(2,1)S(1)} copy-done((bf16[2,316,128]{2,1,0:T(8,128)(2,1)S(1)}, bf16[2,316,128]{2,1,0:T(8,128)(2,1)}, u32[]{:S(2)}) %copy-start.3) | copy-done | bytes 161816
  25.4 0.0 copy-start.11
  25.4 1.2 %copy-done.11 = bf16[2,16,128,128]{3,2,1,0:T(8,128)(2,1)S(1)} copy-done((bf16[2,16,128,128]{3,2,1,0:T(8,128)(2,1)S(1)}, bf16[2,16,128,128]{3,2,1,0:T(8,128)(2,1)}, u32[]{:S(2)}) %copy-start.11) | copy-done | bytes 1048600
  26.6 0.0 copy-start.9
  26.6 7.8 %side.1 = (f32[2,2048,128]{2,1,0:T(8,128)S(1)}, bf16[16,64,128]{2,1,0:T(8,128)(2,1)S(1)}) custom-call(bf16[2,16,128,128]{3,2,1,0:T(8,128)(2,1)S(1)} %copy-done.11, s32[16,48]{1,0:T(8,128)S(1)} %copy-done.13, s32[16,48]{1,0:T(8,128)S(1)} %copy-done.15, bf16[2,316,128]{2,1,0:T(8,128)(2,1)S(1)} %copy-done.3, s32[64,16]{1,0:T(8,128)S(1)} %copy.14.par_source, ...), custom_call_target="tpu_custom_call" | custom-call | flops 4000000000 | bytes 12000000 | tf_op jit(solution)/shard_map/side/pallas_call | solution.py:381
  34.4 0.0 copy-start
  34.5 0.7 copy-done
  35.1 8.7 %all-to-all-done.1.received = bf16[32,160,128]{2,1,0:T(8,128)(2,1)S(1)} async-done(((bf16[32,160,128]{2,1,0:T(8,128)(2,1)}), bf16[32,160,128]{2,1,0:T(8,128)(2,1)S(1)}, u32[]{:S(2)}, u32[]{:S(2)}) %all-to-all-start.1) | async-done | bytes 1310752 | tf_op jit(solution)/shard_map/all_to_all | solution.py:379
  43.9 0.0 copy-done.9
  43.9 0.0 copy-start.1
  43.9 0.9 %copy-done.1 = bf16[16,64,128]{2,1,0:T(8,128)(2,1)S(1)} copy-done((bf16[16,64,128]{2,1,0:T(8,128)(2,1)S(1)}, bf16[16,64,128]{2,1,0:T(8,128)(2,1)}, u32[]{:S(2)}) %copy-start.1) | copy-done | bytes 262168
  44.8 5.0 %middle.1 = bf16[32,192,128]{2,1,0:T(8,128)(2,1)S(1)} custom-call(s32[4]{0:T(128)S(1)} %copy-done.9, bf16[32,160,128]{2,1,0:T(8,128)(2,1)S(1)} %all-to-all-done.1.received, bf16[32,64,128]{2,1,0:T(8,128)(2,1)} %copy-done.16, bf16[16,64,128]{2,1,0:T(8,128)(2,1)S(1)} %copy-done.1), custom_call_target="tpu_custom_call" | custom-call | flops 800000000 | bytes 4000000 | tf_op jit(solution)/shard_map/middle/pallas_call | solution.py:412
  49.8 0.0 copy-start.5
  49.8 0.0 copy-start.7
  49.8 26.7 %all_to_all.15.received = bf16[32,192,128]{2,1,0:T(8,128)(2,1)S(1)} all-to-all(bf16[32,192,128]{2,1,0:T(8,128)(2,1)S(1)} %middle.1), channel_id=1, replica_groups=mesh['illum'=8,'box'=32] {'box'}, dimensions={0} | all-to-all | bytes 3145728 | tf_op jit(solution)/shard_map/all_to_all | solution.py:431
  76.5 0.0 copy-done.5
  76.5 0.0 copy-done.7
  76.5 5.1 %down.1 = f32[2,2,8,128,128]{4,3,2,1,0:T(8,128)} custom-call(bf16[32,192,128]{2,1,0:T(8,128)(2,1)S(1)} %all_to_all.15.received, f32[2,2,8,128,128]{4,3,2,1,0:T(8,128)S(1)} %bitcast.3, bf16[128,512]{1,0:T(8,128)(2,1)S(1)} %copy-done.5, f32[8,512]{1,0:T(8,128)S(1)} %copy-done.7), custom_call_target="tpu_custom_call" | custom-call | flops 1200000000 | bytes 6000000 | tf_op jit(solution)/shard_map/down/pallas_call | solution.py:438
  (1 shorter events, 0.0 us)
Async XLA Ops:
  0.9 0.9 %copy-start.4 = (bf16[128,512]{1,0:T(8,128)(2,1)S(1)}, bf16[128,512]{1,0:T(8,128)(2,1)}, u32[]{:S(2)}) copy-start(bf16[128,512]{1,0:T(8,128)(2,1)} %interp.3) | copy-start | bytes 393220
  1.8 0.7 copy-start.6
  2.6 0.7 copy-start.8
  3.2 1.2 %copy-start.10 = (bf16[2,16,128,128]{3,2,1,0:T(8,128)(2,1)S(1)}, bf16[2,16,128,128]{3,2,1,0:T(8,128)(2,1)}, u32[]{:S(2)}) copy-start(bf16[2,16,128,128]{3,2,1,0:T(8,128)(2,1)} %patterns.3) | copy-start | bytes 3145732
  4.4 0.7 copy-start.12
  5.1 0.7 copy-start.14
  5.8 8.1 %copy-start.2 = (bf16[2,316,128]{2,1,0:T(8,128)(2,1)}, bf16[2,316,128]{2,1,0:T(8,128)(2,1)S(1)}, u32[]{:S(2)}) copy-start(bf16[2,316,128]{2,1,0:T(8,128)(2,1)S(1)} %copy.12.table) | copy-start | bytes 485380
  14.7 0.8 copy-start.16
  14.7 9.4 %copy-start.18 = (s32[64,16]{0,1:T(8,128)S(1)}, s32[64,16]{0,1:T(8,128)}, u32[]{:S(2)}) copy-start(s32[64,16]{0,1:T(8,128)} %param.20) | copy-start | bytes 12292
  14.7 9.5 %copy-start.19 = (s32[64,16]{0,1:T(8,128)S(1)}, s32[64,16]{0,1:T(8,128)}, u32[]{:S(2)}) copy-start(s32[64,16]{0,1:T(8,128)} %param.21) | copy-start | bytes 12292
  14.7 9.5 %copy-start.20 = (s32[64,16]{0,1:T(8,128)S(1)}, s32[64,16]{0,1:T(8,128)}, u32[]{:S(2)}) copy-start(s32[64,16]{0,1:T(8,128)} %param.22) | copy-start | bytes 12292
  14.7 9.6 %copy-start.17 = (bf16[2,316,512]{2,0,1:T(2,128)(2,1)S(1)}, bf16[2,316,512]{2,0,1:T(2,128)(2,1)}, u32[]{:S(2)}) copy-start(bf16[2,316,512]{2,0,1:T(2,128)(2,1)} %param.23) | copy-start | bytes 1941508
  14.7 9.7 %copy-start.13 = (s32[16,48]{1,0:T(8,128)S(1)}, s32[16,48]{1,0:T(8,128)}, u32[]{:S(2)}) copy-start(s32[16,48]{1,0:T(8,128)} %index.3) | copy-start | bytes 9220
  14.8 9.7 %copy-start.15 = (s32[16,48]{1,0:T(8,128)S(1)}, s32[16,48]{1,0:T(8,128)}, u32[]{:S(2)}) copy-start(s32[16,48]{1,0:T(8,128)} %mask.3) | copy-start | bytes 9220
  15.5 28.4 %all-to-all-start.1 = ((bf16[32,160,128]{2,1,0:T(8,128)(2,1)}), bf16[32,160,128]{2,1,0:T(8,128)(2,1)S(1)}, u32[]{:S(2)}, u32[]{:S(2)}) async-start(bf16[32,160,128]{2,1,0:T(8,128)(2,1)} %get-tuple-element.15), calls=%async_computation.1 | async-start | bytes 2621440 | tf_op jit(solution)/shard_map/all_to_all | solution.py:379
  24.5 0.9 %copy-start.3 = (bf16[2,316,128]{2,1,0:T(8,128)(2,1)S(1)}, bf16[2,316,128]{2,1,0:T(8,128)(2,1)}, u32[]{:S(2)}) copy-start(bf16[2,316,128]{2,1,0:T(8,128)(2,1)} %copy-done.2) | copy-start | bytes 485380
  25.4 1.2 %copy-start.11 = (bf16[2,16,128,128]{3,2,1,0:T(8,128)(2,1)S(1)}, bf16[2,16,128,128]{3,2,1,0:T(8,128)(2,1)}, u32[]{:S(2)}) copy-start(bf16[2,16,128,128]{3,2,1,0:T(8,128)(2,1)} %patterns.3) | copy-start | bytes 3145732
  26.6 17.3 %copy-start.9 = (s32[4]{0:T(128)S(1)}, s32[4]{0:T(128)}, u32[]{:S(2)}) copy-start(s32[4]{0:T(128)} %owner.3) | copy-start | bytes 52
  34.4 0.7 copy-start
  43.9 1.0 %copy-start.1 = (bf16[16,64,128]{2,1,0:T(8,128)(2,1)S(1)}, bf16[16,64,128]{2,1,0:T(8,128)(2,1)}, u32[]{:S(2)}) copy-start(bf16[16,64,128]{2,1,0:T(8,128)(2,1)} %copy-done) | copy-start | bytes 786436
  49.8 26.7 %copy-start.5 = (bf16[128,512]{1,0:T(8,128)(2,1)S(1)}, bf16[128,512]{1,0:T(8,128)(2,1)}, u32[]{:S(2)}) copy-start(bf16[128,512]{1,0:T(8,128)(2,1)} %interp.3) | copy-start | bytes 393220
  49.8 26.7 %copy-start.7 = (f32[8,512]{1,0:T(8,128)S(1)}, f32[8,512]{1,0:T(8,128)}, u32[]{:S(2)}) copy-start(f32[8,512]{1,0:T(8,128)} %angle.3) | copy-start | bytes 49156
